TPU v7x, 256 devices: a whole 4x4x8 slice. The times are simulated.
256 devices in a mesh: wide: 32 (over y, x, core), narrow: 8 (over z).
Axes of the slice: x: 4, y: 4, z: 8, core: 2. Of those that a mesh axis runs over, the one named last changes fastest.
Arguments:
- section_state: bfloat16 [24, 4096, 4096], P(None, 'wide', 'narrow'), may hold values from -6 to 6
- cotangent: bfloat16 [24, 4096, 4096], P(None, 'wide', 'narrow'), may hold values from -6 to 6
- bypass_weight: bfloat16 [24, 24], replicated, may hold values from -1.25 to 1.25
- bias: float32 [24], replicated, may hold values from -3 to 3
- spectral_weight: float32 [2, 24, 24, 4096], P(None, None, None, ('wide', 'narrow')), may hold values from -36 to 36
Outputs:
- section_slope: bfloat16 [24, 4096, 4096], P(None, 'wide', 'narrow')
- state_grad: bfloat16 [24, 4096, 4096], P(None, 'wide', 'narrow')
- weight_grad: float32 [2, 24, 24, 4096], P(None, None, None, ('wide', 'narrow'))
All inputs are finite; a program needn't handle non-finite values.
Results may differ from a plain program's by a relative error of at most 0.007.
Values sent between devices are 32-bit elements; how exact they have to be, the bound alone decides.
A program may use at most 128 MiB of HBM per device.

v0:
```python
import math

import jax
import jax.numpy as jnp
import ml_dtypes
import numpy as np
from jax import lax
from jax.experimental import pallas as pl
from jax.experimental.pallas import tpu as pltpu
from jax.sharding import PartitionSpec as P

GRID = 4096
C = 24
MX = 64
MY = 64
WIDE = 32
NARROW = 8
PLANE = 16
ROWS = GRID // WIDE
COLS = GRID // NARROW
GROUPS = C // 8
SLAB = 16
MESH = pl.DeviceIdType.MESH
F32 = jnp.float32
BF16 = jnp.bfloat16


def split_np(values):
    high = values.astype(ml_dtypes.bfloat16)
    low = (values - high.astype(np.float64)).astype(ml_dtypes.bfloat16)
    return high, low


def column_tables():
    m = np.arange(MY)
    phase = (m[None, :] * np.arange(GRID)[:, None]) % GRID * (2.0 * math.pi / GRID)
    cos_y = np.cos(phase).astype(np.float32).reshape(GRID, 4, 1, 16)
    sin_y = np.sin(phase).astype(np.float32).reshape(GRID, 4, 1, 16)
    with_cos = np.concatenate([cos_y, -sin_y], axis=2).reshape(GRID, 128)
    with_sin = np.concatenate([-sin_y, -cos_y], axis=2).reshape(GRID, 128)
    basis = np.concatenate([with_cos, with_sin], axis=1).astype(ml_dtypes.bfloat16)
    basis = basis.reshape(NARROW, COLS, 256)
    return basis, np.ascontiguousarray(basis.transpose(0, 2, 1))


def row_tables():
    r = np.arange(MX)
    core, plane, low = r // 32, (r // 2) % 16, r % 2
    k = 4 * plane + 2 * core + low
    freq = np.where(k < MX // 2, k, k - MX)
    phase = (freq[:, None] * np.arange(GRID)[None, :]) % GRID * (2.0 * math.pi / GRID)
    cos_x = np.cos(phase).reshape(MX, WIDE, ROWS).transpose(1, 0, 2)
    sin_x = np.sin(phase).reshape(MX, WIDE, ROWS).transpose(1, 0, 2)
    both = np.concatenate([cos_x, sin_x], axis=2)
    high, low = split_np(both)
    down = np.concatenate([high, low], axis=1).astype(np.float64) / GRID
    down = down.astype(ml_dtypes.bfloat16)
    high_t, low_t = high.transpose(0, 2, 1), low.transpose(0, 2, 1)
    up = np.ascontiguousarray(np.concatenate([high_t, high_t, low_t], axis=2))
    return down, up


def split(values):
    high = values.astype(BF16)
    return high, (values - high.astype(F32)).astype(BF16)


def dot(a, b):
    return jnp.dot(a, b, preferred_element_type=F32)


def rows_down(part, down, store):
    stacked = jnp.concatenate([part[:, :128], part[:, 128:]], axis=0)
    high, low = split(stacked)
    four = dot(down, jnp.concatenate([high, low], axis=1))
    store(four[:64, :128] + (four[:64, 128:] + four[64:, :128]))


def lanes():
    return lax.broadcasted_iota(jnp.int32, (8, 128), 1)


def roll(tile, shift):
    return pltpu.roll(tile, shift % 128, 1)


def place():
    wide = lax.axis_index("wide")
    z = lax.axis_index("narrow")
    return lax.div(wide, 2), lax.rem(wide, 2), z


def greet():
    plane, core, z = place()
    barrier = pltpu.get_barrier_semaphore()

    def to_plane(d, carry):
        t = lax.rem(plane + d, PLANE)
        pl.semaphore_signal(barrier, inc=1, device_id=(t * 2 + core, z), device_id_type=MESH)
        return carry

    def to_ring(d, carry):
        t = lax.rem(z + d, NARROW)
        pl.semaphore_signal(
            barrier, inc=1, device_id=(plane * 2 + core, t), device_id_type=MESH
        )
        return carry

    pl.semaphore_signal(
        barrier, inc=1, device_id=(plane * 2 + 1 - core, z), device_id_type=MESH
    )
    lax.fori_loop(1, PLANE, to_plane, 0)
    lax.fori_loop(1, NARROW, to_ring, 0)


def greeted():
    pl.semaphore_wait(pltpu.get_barrier_semaphore(), 1 + (PLANE - 1) + (NARROW - 1))


def remote(src, dst, send, recv, wide, z):
    return pltpu.make_async_remote_copy(
        src_ref=src,
        dst_ref=dst,
        send_sem=send,
        recv_sem=recv,
        device_id=(wide, z),
        device_id_type=MESH,
    )


COMM_SCRATCH = [
    pltpu.VMEM((GROUPS, 256, 128), F32),
    pltpu.VMEM((GROUPS, PLANE, 16, 128), F32),
    pltpu.VMEM((NARROW, 8, 128), F32),
    pltpu.VMEM((NARROW, 8, 128), F32),
    pltpu.VMEM((8, 128), F32),
    pltpu.VMEM((NARROW, 8, 128), F32),
    pltpu.VMEM((MX * C, 128), F32),
    pltpu.SemaphoreType.DMA((2, GROUPS)),
    pltpu.SemaphoreType.DMA((1 + GROUPS,)),
    pltpu.SemaphoreType.DMA((2,)),
    pltpu.SemaphoreType.DMA((2,)),
    pltpu.SemaphoreType.DMA((1 + PLANE,)),
    pltpu.SemaphoreType.DMA((2,)),
]
PAIR, SLOTS, PACKED, RING, OWN, FINAL, MODES = range(7)
PAIR_SEM, PLANE_SEM, RING_SEM, GATHER_RING, GATHER_PLANE, GATHER_PAIR = range(7, 13)


def pair_copy(parts, comm, g):
    plane, core, z = place()
    sems = comm[PAIR_SEM]
    return remote(
        parts.at[g, 1 - core],
        comm[PAIR].at[g],
        sems.at[0, g],
        sems.at[1, g],
        plane * 2 + 1 - core,
        z,
    )


def arrived(ref, sem):
    pltpu.make_async_copy(ref, ref, sem).wait()


def ring_sends(copy, z):
    for d in (4, 3, 5, 2, 6, 1, 7):
        copy(lax.rem(z + d, NARROW)).start()


def plane_order():
    steps = [(dy, dx) for dy in range(4) for dx in range(4) if dy or dx]
    hops = (0, 1, 2, 1)
    return sorted(steps, key=lambda step: -hops[step[0]] - hops[step[1]])


def plane_targets(plane):
    y, x = lax.div(plane, 4), lax.rem(plane, 4)
    return [lax.rem(y + dy, 4) * 4 + lax.rem(x + dx, 4) for dy, dx in plane_order()]


def reduce_scatter(parts, comm, meanwhile=None):
    pair, slots, packed, ring = comm[PAIR], comm[SLOTS], comm[PACKED], comm[RING]
    plane_sems, ring_sems = comm[PLANE_SEM], comm[RING_SEM]
    plane, core, z = place()
    targets = plane_targets(plane)

    for g in range(GROUPS):
        pair_copy(parts, comm, g).wait_recv()
        pair[g] = pair[g] + parts[g, core]
        for t in targets:
            remote(
                pair.at[g, pl.ds(pl.multiple_of(t * 16, 16), 16)],
                slots.at[g, plane],
                plane_sems.at[0],
                plane_sems.at[1 + g],
                t * 2 + core,
                z,
            ).start()
        slots[g, plane] = pair[g, pl.ds(pl.multiple_of(plane * 16, 16), 16)]

    if meanwhile is not None:
        meanwhile()

    sums = []
    for g in range(GROUPS):
        arrived(slots.at[g, pl.ds(0, PLANE - 1)], plane_sems.at[1 + g])
        sums.append(jnp.sum(slots[g], axis=0))

    lane_group = lanes() // 32
    for low in range(2):
        for quarter in range(4):
            tile = jnp.zeros((8, 128), F32)
            for g in range(GROUPS):
                moved = roll(sums[g][low * 8 : low * 8 + 8], 32 * (g - quarter))
                tile = jnp.where(lane_group == g, moved, tile)
            packed[low * 4 + quarter] = tile

    def ring_copy(t):
        return remote(
            packed.at[t], ring.at[z], ring_sems.at[0], ring_sems.at[1], plane * 2 + core, t
        )

    ring_sends(ring_copy, z)
    ring[z] = packed[z]
    arrived(ring.at[pl.ds(0, NARROW - 1)], ring_sems.at[1])
    return jnp.sum(ring[...], axis=0)


def reduce_scatter_sent(parts, comm):
    for g in range(GROUPS):
        pair_copy(parts, comm, g).wait_send()
    for g in range(GROUPS):
        arrived(comm[SLOTS].at[g, pl.ds(0, PLANE - 1)], comm[PLANE_SEM].at[0])
    arrived(comm[RING].at[pl.ds(0, NARROW - 1)], comm[RING_SEM].at[0])


def pack(real, imag):
    pad = jnp.zeros((8, 96), F32)
    lane_group = lanes() // 32
    tile = jnp.zeros((8, 128), F32)
    for g in range(GROUPS):
        rows = slice(g * 8, g * 8 + 8)
        wide_tile = jnp.concatenate([real[rows], imag[rows], pad], axis=1)
        tile = jnp.where(lane_group == g, roll(wide_tile, 32 * g), tile)
    return tile


def all_gather(tile, comm, meanwhile=None):
    own, ring, modes = comm[OWN], comm[FINAL], comm[MODES]
    ring_sems, plane_sems, pair_sems = comm[GATHER_RING], comm[GATHER_PLANE], comm[GATHER_PAIR]
    plane, core, z = place()
    own[...] = tile

    def ring_copy(t):
        return remote(own, ring.at[z], ring_sems.at[0], ring_sems.at[1], plane * 2 + core, t)

    ring_sends(ring_copy, z)
    ring[z] = tile
    arrived(ring.at[pl.ds(0, NARROW - 1)], ring_sems.at[1])

    def chunk(which, j):
        return modes.at[pl.ds(pl.multiple_of((which * PLANE + j) * 48, 48), 48)]

    lane_group = lanes() // 32
    blocks = []
    for low in range(2):
        for g in range(GROUPS):
            block = jnp.zeros((8, 128), F32)
            for quarter in range(4):
                moved = roll(ring[low * 4 + quarter], 32 * (quarter - g))
                block = jnp.where(lane_group == quarter, moved, block)
            blocks.append(block)
    modes[pl.ds(pl.multiple_of((core * PLANE + plane) * 48, 48), 48)] = jnp.concatenate(
        blocks, axis=0
    )

    def plane_copy(t, j):
        return remote(
            chunk(core, j), chunk(core, j), plane_sems.at[0], plane_sems.at[1 + j], t * 2 + core, z
        )

    def pair_forward(j):
        return remote(
            chunk(core, j),
            chunk(core, j),
            pair_sems.at[0],
            pair_sems.at[1],
            plane * 2 + 1 - core,
            z,
        )

    targets = plane_targets(plane)
    for t in targets:
        plane_copy(t, plane).start()
    pair_forward(plane).start()
    if meanwhile is not None:
        meanwhile()
    for j in reversed(targets):
        plane_copy(plane, j).wait_recv()
        pair_forward(j).start()
    other = modes.at[pl.ds(pl.multiple_of((1 - core) * PLANE * 48, 48), PLANE * 48)]
    arrived(other, pair_sems.at[1])
    arrived(other, pair_sems.at[0])
    arrived(modes.at[pl.ds(0, (PLANE - 1) * 48)], plane_sems.at[0])
    arrived(ring.at[pl.ds(0, NARROW - 1)], ring_sems.at[0])


def expand(modes, up, out_ref):
    for c in range(0, C, 2):
        both = jnp.concatenate(
            [modes[pl.ds(c + i, MX, stride=C), :] for i in range(2)], axis=1
        )
        high, low = split(both)
        rows = dot(up, jnp.concatenate([high, low, high], axis=0))
        for i in range(2):
            at = slice(i * 128, i * 128 + 128)
            out_ref[c + i] = jnp.concatenate([rows[:128, at], rows[128:, at]], axis=1).astype(
                BF16
            )


def unpack(tile):
    real = [roll(tile, -32 * g) for g in range(GROUPS)]
    imag = [roll(tile, -32 * g - 16) for g in range(GROUPS)]
    return real, imag


def mode_weight():
    z = lax.axis_index("narrow")
    first = jnp.logical_and(lanes() % 16 == 0, lax.rem(z, 4) == 0)
    return jnp.where(first, 1.0, 2.0).astype(F32)


def channel_map(weight, transpose):
    size = C * SLAB
    pick = (
        lax.broadcasted_iota(jnp.int32, (size, C), 0) // SLAB
        == lax.broadcasted_iota(jnp.int32, (size, C), 1)
    ).astype(BF16)
    first = lax.dot_general(
        pick, weight, (((1,), (0 if not transpose else 1,)), ((), ())), preferred_element_type=F32
    ).astype(BF16)
    full = lax.dot_general(first, pick, (((1,), (1,)), ((), ())), preferred_element_type=F32)
    same = (
        lax.broadcasted_iota(jnp.int32, (size, size), 0) % SLAB
        == lax.broadcasted_iota(jnp.int32, (size, size), 1) % SLAB
    )
    return jnp.where(same, full, 0.0).astype(BF16)


def slab(s):
    return pl.ds(pl.multiple_of(s * SLAB, SLAB), SLAB)


def mix(weights, spectrum):
    real, imag = unpack(spectrum)
    mixed_real = jnp.zeros((C, 16), F32)
    mixed_imag = jnp.zeros((C, 16), F32)
    for i in range(C):
        s_real = real[i // 8][i % 8 : i % 8 + 1, :16]
        s_imag = imag[i // 8][i % 8 : i % 8 + 1, :16]
        w_real, w_imag = weights[0, i], weights[1, i]
        mixed_real += w_real * s_real - w_imag * s_imag
        mixed_imag += w_real * s_imag + w_imag * s_real
    return pack(mixed_real, mixed_imag)


def columns(tile):
    real, imag = unpack(tile)
    return (
        jnp.concatenate([part[:, :16] for part in real], axis=0),
        jnp.concatenate([part[:, :16] for part in imag], axis=0),
    )


def mix_back(weights, cot):
    y_real, y_imag = columns(cot)
    pulled_real, pulled_imag = [], []
    for g in range(GROUPS):
        w_real, w_imag = weights[0, g * 8 : g * 8 + 8], weights[1, g * 8 : g * 8 + 8]
        pulled_real.append(jnp.sum(w_real * y_real[None] + w_imag * y_imag[None], axis=1))
        pulled_imag.append(jnp.sum(w_real * y_imag[None] - w_imag * y_real[None], axis=1))
    return pack(jnp.concatenate(pulled_real, axis=0), jnp.concatenate(pulled_imag, axis=0))


def weight_terms(spectrum, cot, weight_grad):
    x_real, x_imag = unpack(spectrum)
    c_real, c_imag = columns(cot)
    for i in range(C):
        s_real = x_real[i // 8][i % 8 : i % 8 + 1, :16]
        s_imag = x_imag[i // 8][i % 8 : i % 8 + 1, :16]
        weight_grad[0, i] = s_real * c_real + s_imag * c_imag
        weight_grad[1, i] = s_real * c_imag - s_imag * c_real


def map_channels(mixer, source, target):
    size = C * SLAB

    def step(s, carry):
        value = dot(mixer[...], source[:, slab(s), :].reshape(size, COLS))
        target[:, slab(s), :] = value.reshape(C, SLAB, COLS)
        return carry

    lax.fori_loop(0, ROWS // SLAB, step, 0)


def main_kernel(
    state_hbm, cotangent_hbm, weight, bias, weights, basis_hbm, basis_t_hbm, down_hbm, up_hbm,
    slope, linear, back_rows, weight_grad,
    state, cotangent, seed, rows, back, basis, basis_t, down, up, mixer, mixer_t,
    parts, back_parts, load_sems, *comms,
):
    comm, back_comm = comms[: len(COMM_SCRATCH)], comms[len(COMM_SCRATCH) :]
    plane, core, z = place()
    wide = plane * 2 + core
    size = C * SLAB
    loads = [
        pltpu.make_async_copy(basis_hbm.at[z], basis, load_sems.at[0]),
        pltpu.make_async_copy(down_hbm.at[wide], down, load_sems.at[1]),
    ]
    for g in range(GROUPS):
        at = pl.ds(g * 8, 8)
        loads.append(pltpu.make_async_copy(state_hbm.at[at], state.at[at], load_sems.at[2 + g]))
    loads += [
        pltpu.make_async_copy(up_hbm.at[wide], up, load_sems.at[5]),
        pltpu.make_async_copy(basis_t_hbm.at[z], basis_t, load_sems.at[6]),
        pltpu.make_async_copy(cotangent_hbm, cotangent, load_sems.at[7]),
    ]
    for load in loads:
        load.start()
    greet()
    for load in loads[:2]:
        load.wait()

    def send_parts(source, to, peers, g):
        for row in range(8):

            def store(value, row=row):
                to[g, 0, pl.ds(row, 32, stride=8), :] = value[:32]
                to[g, 1, pl.ds(row, 32, stride=8), :] = value[32:]

            rows_down(source(g * 8 + row), down[...], store)
        if g == 0 and peers is comm:
            greeted()
        pair_copy(to, peers, g).start()

    for g in range(GROUPS):
        loads[2 + g].wait()
        send_parts(lambda c: dot(state[c], basis[...]), parts, comm, g)

    def bypass():
        mixer[...] = channel_map(weight[...], False)
        mixer_t[...] = channel_map(weight[...], True)
        map_channels(mixer_t, state, linear)

    spectrum = reduce_scatter(parts, comm, bypass)
    tile = mix(weights, spectrum) * (mode_weight() * (1.0 / GRID))
    for load in loads[5:]:
        load.wait()
    all_gather(tile, comm, lambda: reduce_scatter_sent(parts, comm))
    expand(comm[MODES], up[...], rows)

    def point(s, carry):
        linear[:, slab(s), :] += dot(
            rows[:, slab(s), :].reshape(size, 256), basis_t[...]
        ).reshape(C, SLAB, COLS)

        def channel(c, carry):
            value = linear[c, slab(s), :] + bias[c]
            cdf = 0.5 * (1.0 + lax.erf(value * (1.0 / math.sqrt(2.0))))
            density = jnp.exp(-0.5 * value * value) * (1.0 / math.sqrt(2.0 * math.pi))
            slope[c, slab(s), :] = (value * cdf).astype(BF16)
            seed[c, slab(s), :] = (
                cotangent[c, slab(s), :].astype(F32) * (cdf + value * density)
            ).astype(BF16)
            return carry

        lax.fori_loop(0, C, channel, 0)
        back[:, slab(s), :] = dot(seed[:, slab(s), :].reshape(size, COLS), basis[...]).reshape(
            C, SLAB, 256
        )
        return carry

    lax.fori_loop(0, ROWS // SLAB, point, 0)
    for g in range(GROUPS):
        send_parts(lambda c: back[c], back_parts, back_comm, g)
    cot = reduce_scatter(
        back_parts, back_comm, lambda: map_channels(mixer, seed, linear)
    ) * mode_weight()

    def meanwhile():
        weight_terms(spectrum, cot, weight_grad)
        reduce_scatter_sent(back_parts, back_comm)

    all_gather(mix_back(weights, cot) * (1.0 / GRID), back_comm, meanwhile)
    expand(back_comm[MODES], up[...], back_rows)


def final_kernel(
    slope, linear, rows, basis_t_hbm, slope_out, grad_out, basis_t, grad, sems, slope_sem, load_sem
):
    z = lax.axis_index("narrow")
    slope_copy = pltpu.make_async_copy(slope, slope_out, slope_sem)
    slope_copy.start()
    load = pltpu.make_async_copy(basis_t_hbm.at[z], basis_t, load_sem)
    load.start()
    load.wait()
    size = C * SLAB
    copies = []
    for s in range(ROWS // SLAB):
        at = pl.ds(s * SLAB, SLAB)
        value = linear[:, at, :].reshape(size, COLS) + dot(
            rows[:, at, :].reshape(size, 256), basis_t[...]
        )
        grad[:, at, :] = value.astype(BF16).reshape(C, SLAB, COLS)
        copy = pltpu.make_async_copy(grad.at[:, at, :], grad_out.at[:, at, :], sems.at[s])
        copy.start()
        copies.append(copy)
    for copy in copies:
        copy.wait()
    slope_copy.wait()


VMEM = pl.BlockSpec(memory_space=pltpu.VMEM)
HBM = pl.BlockSpec(memory_space=pltpu.HBM)
SMEM = pl.BlockSpec(memory_space=pltpu.SMEM)


def params(megabytes, **more):
    return pltpu.CompilerParams(vmem_limit_bytes=megabytes * 1024 * 1024, **more)


def solution(mesh):
    basis_np, basis_t_np = column_tables()
    down_np, up_np = row_tables()

    def per_device(section_state, cotangent, bypass_weight, bias, spectral_weight):
        basis_all, basis_t_all, down_all, up_all, section_state, cotangent = (
            pltpu.with_memory_space_constraint(jnp.asarray(array), pltpu.HBM)
            for array in (basis_np, basis_t_np, down_np, up_np, section_state, cotangent)
        )
        rows_shape = jax.ShapeDtypeStruct((C, ROWS, 256), BF16)
        field = jax.ShapeDtypeStruct((C, ROWS, COLS), BF16)
        wide_field = jax.ShapeDtypeStruct((C, ROWS, COLS), F32)

        slope, linear, rows, weight_grad = pl.pallas_call(
            main_kernel,
            out_shape=(field, wide_field, rows_shape, jax.ShapeDtypeStruct((2, C, C, 16), F32)),
            in_specs=[HBM, HBM, VMEM, SMEM, VMEM, HBM, HBM, HBM, HBM],
            out_specs=(VMEM, VMEM, VMEM, VMEM),
            scratch_shapes=[
                pltpu.VMEM((C, ROWS, COLS), BF16),
                pltpu.VMEM((C, ROWS, COLS), BF16),
                pltpu.VMEM((C, ROWS, COLS), BF16),
                pltpu.VMEM((C, ROWS, 256), BF16),
                pltpu.VMEM((C, ROWS, 256), F32),
                pltpu.VMEM((COLS, 256), BF16),
                pltpu.VMEM((256, COLS), BF16),
                pltpu.VMEM((128, 256), BF16),
                pltpu.VMEM((256, 192), BF16),
                pltpu.VMEM((C * SLAB, C * SLAB), BF16),
                pltpu.VMEM((C * SLAB, C * SLAB), BF16),
                pltpu.VMEM((GROUPS, 2, 256, 128), F32),
                pltpu.VMEM((GROUPS, 2, 256, 128), F32),
                pltpu.SemaphoreType.DMA((8,)),
                *COMM_SCRATCH,
                *COMM_SCRATCH,
            ],
            compiler_params=params(26, collective_id=0, has_side_effects=True),
            name="section",
        )(
            section_state, cotangent, bypass_weight, bias, spectral_weight,
            basis_all, basis_t_all, down_all, up_all,
        )

        slope, state_grad = pl.pallas_call(
            final_kernel,
            out_shape=(field, field),
            in_specs=[VMEM, VMEM, VMEM, HBM],
            out_specs=(HBM, HBM),
            scratch_shapes=[
                pltpu.VMEM((256, COLS), BF16),
                pltpu.VMEM((C, ROWS, COLS), BF16),
                pltpu.SemaphoreType.DMA((ROWS // SLAB,)),
                pltpu.SemaphoreType.DMA,
                pltpu.SemaphoreType.DMA,
            ],
            compiler_params=params(16),
            name="state_gradient",
        )(slope, linear, rows, basis_t_all)
        return slope, state_grad, weight_grad

    split_modes = P(None, None, None, ("wide", "narrow"))
    tiles = P(None, "wide", "narrow")
    return jax.shard_map(
        per_device,
        mesh=mesh,
        in_specs=(tiles, tiles, P(), P(), split_modes),
        out_specs=(tiles, tiles, split_modes),
        check_vma=False,
    )
```

profile of v0, /device:TPU:1, one launch (start us, length us, event | category | flops | bytes accessed | tf_op | source)
XLA Modules:
  0.0 84.9 jit_solution(97876769476631427)
XLA Ops:
  0.6 1.2 %copy.12.weights = f32[2,24,24,16]{3,2,1,0:T(8,128)S(1)} copy(f32[2,24,24,16]{2,3,1,0:T(8,128)} %param.13) | data formatting | bytes 147456 | tf_op args[4]
  1.9 0.0 copy-start
  1.9 0.7 copy-done
  2.6 0.0 copy-start.1
  2.6 0.7 copy-done.1
  3.2 77.6 %section.1 = (bf16[24,128,512]{2,1,0:T(8,128)(2,1)S(1)}, f32[24,128,512]{2,1,0:T(8,128)S(1)}, bf16[24,128,256]{2,1,0:T(8,128)(2,1)S(1)}, f32[2,24,24,16]{3,2,1,0:T(8,128)S(1)}) custom-call(bf16[24,128,512]{2,1,0:T(8,128)(2,1)} %state_hbm.1, bf16[24,128,512]{2,1,0:T(8,128)(2,1)} %cotangent_hbm.1, bf16[24,24]{1,0:T(8,128)(2,1)S(1)} %copy-done, ...), custom_call_target="tpu_custom_call" | custom-call | tf_op jit(solution)/shard_map/section/pallas_call | solution.py:548
  80.8 3.1 %state_gradient.1 = (bf16[24,128,512]{2,1,0:T(8,128)(2,1)}, bf16[24,128,512]{2,1,0:T(8,128)(2,1)}) custom-call(bf16[24,128,512]{2,1,0:T(8,128)(2,1)S(1)} %get-tuple-element.9.slope, f32[24,128,512]{2,1,0:T(8,128)S(1)} %get-tuple-element.10.linear, bf16[24,128,256]{2,1,0:T(8,128)(2,1)S(1)} %get-tuple-element.11.rows, ...), custom_call_target="tpu_custom_call" | custom-call | tf_op jit(solution)/shard_map/state_gradient/pallas_call | solution.py:578
  83.9 1.0 %copy.13 = f32[2,24,24,16]{2,3,1,0:T(8,128)} copy(f32[2,24,24,16]{3,2,1,0:T(8,128)S(1)} %get-tuple-element.17) | data formatting | bytes 147456
Async XLA Ops:
  1.9 0.7 copy-start
  2.6 0.7 copy-start.1
where the time goes:
time: 85.1 us; the launch traced here: 84.9 us
  Pallas kernels  80.7 us (95%)
  local copies, waits for them, and re-layouts  3.54 us (4%)
    pallas_call x1, Pallas kernels, per_device(): pl.pallas_call(main_kernel, out_shape=(field, wide_field, rows_shape, jax...  77.6 us
    unnamed x6, local copies, waits for them, and re-layouts  3.54 us
    pallas_call x1, Pallas kernels, per_device(): pl.pallas_call(final_kernel, out_shape=(field, field), in_specs=[VMEM, VM...  3.1 us

commit v1 on v0

--- a/solution.py
+++ b/solution.py
@@ -135,13 +135,13 @@
     pltpu.VMEM((NARROW, 8, 128), F32),
     pltpu.VMEM((8, 128), F32),
     pltpu.VMEM((NARROW, 8, 128), F32),
-    pltpu.VMEM((MX * C, 128), F32),
+    pltpu.VMEM((GROUPS, MX * 8, 128), F32),
     pltpu.SemaphoreType.DMA((2, GROUPS)),
     pltpu.SemaphoreType.DMA((1 + GROUPS,)),
     pltpu.SemaphoreType.DMA((2,)),
     pltpu.SemaphoreType.DMA((2,)),
-    pltpu.SemaphoreType.DMA((1 + PLANE,)),
-    pltpu.SemaphoreType.DMA((2,)),
+    pltpu.SemaphoreType.DMA((1 + GROUPS * PLANE,)),
+    pltpu.SemaphoreType.DMA((1 + GROUPS,)),
 ]
 PAIR, SLOTS, PACKED, RING, OWN, FINAL, MODES = range(7)
 PAIR_SEM, PLANE_SEM, RING_SEM, GATHER_RING, GATHER_PLANE, GATHER_PAIR = range(7, 13)
@@ -180,28 +180,27 @@
     return [lax.rem(y + dy, 4) * 4 + lax.rem(x + dx, 4) for dy, dx in plane_order()]
 
 
-def reduce_scatter(parts, comm, meanwhile=None):
-    pair, slots, packed, ring = comm[PAIR], comm[SLOTS], comm[PACKED], comm[RING]
+def plane_stage(parts, comm, g):
+    pair, slots, plane_sems = comm[PAIR], comm[SLOTS], comm[PLANE_SEM]
+    plane, core, z = place()
+    pair_copy(parts, comm, g).wait_recv()
+    pair[g] = pair[g] + parts[g, core]
+    for t in plane_targets(plane):
+        remote(
+            pair.at[g, pl.ds(pl.multiple_of(t * 16, 16), 16)],
+            slots.at[g, plane],
+            plane_sems.at[0],
+            plane_sems.at[1 + g],
+            t * 2 + core,
+            z,
+        ).start()
+    slots[g, plane] = pair[g, pl.ds(pl.multiple_of(plane * 16, 16), 16)]
+
+
+def reduce_scatter(comm):
+    slots, packed, ring = comm[SLOTS], comm[PACKED], comm[RING]
     plane_sems, ring_sems = comm[PLANE_SEM], comm[RING_SEM]
     plane, core, z = place()
-    targets = plane_targets(plane)
-
-    for g in range(GROUPS):
-        pair_copy(parts, comm, g).wait_recv()
-        pair[g] = pair[g] + parts[g, core]
-        for t in targets:
-            remote(
-                pair.at[g, pl.ds(pl.multiple_of(t * 16, 16), 16)],
-                slots.at[g, plane],
-                plane_sems.at[0],
-                plane_sems.at[1 + g],
-                t * 2 + core,
-                z,
-            ).start()
-        slots[g, plane] = pair[g, pl.ds(pl.multiple_of(plane * 16, 16), 16)]
-
-    if meanwhile is not None:
-        meanwhile()
 
     sums = []
     for g in range(GROUPS):
@@ -247,7 +246,7 @@
     return tile
 
 
-def all_gather(tile, comm, meanwhile=None):
+def all_gather(tile, comm, meanwhile, consume):
     own, ring, modes = comm[OWN], comm[FINAL], comm[MODES]
     ring_sems, plane_sems, pair_sems = comm[GATHER_RING], comm[GATHER_PLANE], comm[GATHER_PAIR]
     plane, core, z = place()
@@ -260,65 +259,83 @@
     ring[z] = tile
     arrived(ring.at[pl.ds(0, NARROW - 1)], ring_sems.at[1])
 
-    def chunk(which, j):
-        return modes.at[pl.ds(pl.multiple_of((which * PLANE + j) * 48, 48), 48)]
-
+    def chunk(g, which, j):
+        return modes.at[g, pl.ds(pl.multiple_of((which * PLANE + j) * 16, 16), 16)]
+
+    def plane_copy(g, t, j):
+        return remote(
+            chunk(g, core, j),
+            chunk(g, core, j),
+            plane_sems.at[0],
+            plane_sems.at[1 + g * PLANE + j],
+            t * 2 + core,
+            z,
+        )
+
+    def pair_forward(g, j):
+        return remote(
+            chunk(g, core, j),
+            chunk(g, core, j),
+            pair_sems.at[0],
+            pair_sems.at[1 + g],
+            plane * 2 + 1 - core,
+            z,
+        )
+
+    targets = plane_targets(plane)
     lane_group = lanes() // 32
-    blocks = []
-    for low in range(2):
-        for g in range(GROUPS):
+    for g in range(GROUPS):
+        blocks = []
+        for low in range(2):
             block = jnp.zeros((8, 128), F32)
             for quarter in range(4):
                 moved = roll(ring[low * 4 + quarter], 32 * (quarter - g))
                 block = jnp.where(lane_group == quarter, moved, block)
             blocks.append(block)
-    modes[pl.ds(pl.multiple_of((core * PLANE + plane) * 48, 48), 48)] = jnp.concatenate(
-        blocks, axis=0
-    )
-
-    def plane_copy(t, j):
-        return remote(
-            chunk(core, j), chunk(core, j), plane_sems.at[0], plane_sems.at[1 + j], t * 2 + core, z
-        )
-
-    def pair_forward(j):
-        return remote(
-            chunk(core, j),
-            chunk(core, j),
-            pair_sems.at[0],
-            pair_sems.at[1],
-            plane * 2 + 1 - core,
-            z,
-        )
-
-    targets = plane_targets(plane)
-    for t in targets:
-        plane_copy(t, plane).start()
-    pair_forward(plane).start()
-    if meanwhile is not None:
-        meanwhile()
-    for j in reversed(targets):
-        plane_copy(plane, j).wait_recv()
-        pair_forward(j).start()
-    other = modes.at[pl.ds(pl.multiple_of((1 - core) * PLANE * 48, 48), PLANE * 48)]
-    arrived(other, pair_sems.at[1])
-    arrived(other, pair_sems.at[0])
-    arrived(modes.at[pl.ds(0, (PLANE - 1) * 48)], plane_sems.at[0])
-    arrived(ring.at[pl.ds(0, NARROW - 1)], ring_sems.at[0])
-
-
-def expand(modes, up, out_ref):
-    for c in range(0, C, 2):
+        modes[g, pl.ds(pl.multiple_of((core * PLANE + plane) * 16, 16), 16)] = jnp.concatenate(
+            blocks, axis=0
+        )
+        for t in targets:
+            plane_copy(g, t, plane).start()
+        pair_forward(g, plane).start()
+    meanwhile()
+
+    def forward(g):
+        for j in reversed(targets):
+            plane_copy(g, plane, j).wait_recv()
+            pair_forward(g, j).start()
+
+    def other(g):
+        return modes.at[g, pl.ds(pl.multiple_of((1 - core) * PLANE * 16, 16), PLANE * 16)]
+
+    forward(0)
+    for g in range(GROUPS):
+        if g + 1 < GROUPS:
+            forward(g + 1)
+        arrived(other(g), pair_sems.at[1 + g])
+        consume(g)
+
+
+def all_gather_sent(comm):
+    modes = comm[MODES]
+    for g in range(GROUPS):
+        arrived(modes.at[g, pl.ds(0, PLANE * 16)], comm[GATHER_PAIR].at[0])
+        arrived(modes.at[g, pl.ds(0, (PLANE - 1) * 16)], comm[GATHER_PLANE].at[0])
+    arrived(comm[FINAL].at[pl.ds(0, NARROW - 1)], comm[GATHER_RING].at[0])
+
+
+def expand(modes, up, g, out_ref):
+    for row in range(0, 8, 2):
         both = jnp.concatenate(
-            [modes[pl.ds(c + i, MX, stride=C), :] for i in range(2)], axis=1
+            [modes[g, pl.ds(row + i, MX, stride=8), :] for i in range(2)], axis=1
         )
         high, low = split(both)
         rows = dot(up, jnp.concatenate([high, low, high], axis=0))
         for i in range(2):
             at = slice(i * 128, i * 128 + 128)
-            out_ref[c + i] = jnp.concatenate([rows[:128, at], rows[128:, at]], axis=1).astype(
-                BF16
-            )
+            out_ref[g * 8 + row + i] = jnp.concatenate(
+                [rows[:128, at], rows[128:, at]], axis=1
+            ).astype(BF16)
 
 
 def unpack(tile):
@@ -391,8 +408,8 @@
     for i in range(C):
         s_real = x_real[i // 8][i % 8 : i % 8 + 1, :16]
         s_imag = x_imag[i // 8][i % 8 : i % 8 + 1, :16]
-        weight_grad[0, i] = s_real * c_real + s_imag * c_imag
-        weight_grad[1, i] = s_real * c_imag - s_imag * c_real
+        weight_grad[0, i] = (s_real * c_real + s_imag * c_imag).T
+        weight_grad[1, i] = (s_real * c_imag - s_imag * c_real).T
 
 
 def map_channels(mixer, source, target):
@@ -407,15 +424,16 @@
 
 
 def main_kernel(
-    state_hbm, cotangent_hbm, weight, bias, weights, basis_hbm, basis_t_hbm, down_hbm, up_hbm,
+    state_hbm, cotangent_hbm, weight_hbm, bias_hbm, weights_hbm,
+    basis_hbm, basis_t_hbm, down_hbm, up_hbm,
     slope, linear, back_rows, weight_grad,
-    state, cotangent, seed, rows, back, basis, basis_t, down, up, mixer, mixer_t,
+    state, cotangent, seed, rows, back, weight, bias, weights_t, weights,
+    basis, basis_t, down, up, mixer, mixer_t,
     parts, back_parts, load_sems, *comms,
 ):
     comm, back_comm = comms[: len(COMM_SCRATCH)], comms[len(COMM_SCRATCH) :]
     plane, core, z = place()
     wide = plane * 2 + core
-    size = C * SLAB
     loads = [
         pltpu.make_async_copy(basis_hbm.at[z], basis, load_sems.at[0]),
         pltpu.make_async_copy(down_hbm.at[wide], down, load_sems.at[1]),
@@ -424,9 +442,12 @@
         at = pl.ds(g * 8, 8)
         loads.append(pltpu.make_async_copy(state_hbm.at[at], state.at[at], load_sems.at[2 + g]))
     loads += [
-        pltpu.make_async_copy(up_hbm.at[wide], up, load_sems.at[5]),
-        pltpu.make_async_copy(basis_t_hbm.at[z], basis_t, load_sems.at[6]),
-        pltpu.make_async_copy(cotangent_hbm, cotangent, load_sems.at[7]),
+        pltpu.make_async_copy(weight_hbm, weight, load_sems.at[5]),
+        pltpu.make_async_copy(weights_hbm, weights_t, load_sems.at[6]),
+        pltpu.make_async_copy(up_hbm.at[wide], up, load_sems.at[7]),
+        pltpu.make_async_copy(basis_t_hbm.at[z], basis_t, load_sems.at[8]),
+        pltpu.make_async_copy(bias_hbm, bias, load_sems.at[9]),
+        pltpu.make_async_copy(cotangent_hbm, cotangent, load_sems.at[10]),
     ]
     for load in loads:
         load.start()
@@ -434,76 +455,90 @@
     for load in loads[:2]:
         load.wait()
 
-    def send_parts(source, to, peers, g):
+    def send_parts(to, peers, g):
         for row in range(8):
 
             def store(value, row=row):
                 to[g, 0, pl.ds(row, 32, stride=8), :] = value[:32]
                 to[g, 1, pl.ds(row, 32, stride=8), :] = value[32:]
 
-            rows_down(source(g * 8 + row), down[...], store)
+            rows_down(back[g * 8 + row], down[...], store)
         if g == 0 and peers is comm:
             greeted()
         pair_copy(to, peers, g).start()
+        if g:
+            plane_stage(to, peers, g - 1)
+
+    def to_columns(source, g):
+        at = slice(g * 8, g * 8 + 8)
+        back[at] = dot(source[at].reshape(8 * ROWS, COLS), basis[...]).reshape(8, ROWS, 256)
 
     for g in range(GROUPS):
         loads[2 + g].wait()
-        send_parts(lambda c: dot(state[c], basis[...]), parts, comm, g)
-
-    def bypass():
-        mixer[...] = channel_map(weight[...], False)
-        mixer_t[...] = channel_map(weight[...], True)
-        map_channels(mixer_t, state, linear)
-
-    spectrum = reduce_scatter(parts, comm, bypass)
-    tile = mix(weights, spectrum) * (mode_weight() * (1.0 / GRID))
+        to_columns(state, g)
+        send_parts(parts, comm, g)
+    plane_stage(parts, comm, GROUPS - 1)
+
     for load in loads[5:]:
         load.wait()
-    all_gather(tile, comm, lambda: reduce_scatter_sent(parts, comm))
-    expand(comm[MODES], up[...], rows)
-
-    def point(s, carry):
-        linear[:, slab(s), :] += dot(
-            rows[:, slab(s), :].reshape(size, 256), basis_t[...]
-        ).reshape(C, SLAB, COLS)
-
-        def channel(c, carry):
-            value = linear[c, slab(s), :] + bias[c]
-            cdf = 0.5 * (1.0 + lax.erf(value * (1.0 / math.sqrt(2.0))))
-            density = jnp.exp(-0.5 * value * value) * (1.0 / math.sqrt(2.0 * math.pi))
-            slope[c, slab(s), :] = (value * cdf).astype(BF16)
-            seed[c, slab(s), :] = (
-                cotangent[c, slab(s), :].astype(F32) * (cdf + value * density)
-            ).astype(BF16)
-            return carry
-
-        lax.fori_loop(0, C, channel, 0)
-        back[:, slab(s), :] = dot(seed[:, slab(s), :].reshape(size, COLS), basis[...]).reshape(
-            C, SLAB, 256
-        )
-        return carry
-
-    lax.fori_loop(0, ROWS // SLAB, point, 0)
-    for g in range(GROUPS):
-        send_parts(lambda c: back[c], back_parts, back_comm, g)
-    cot = reduce_scatter(
-        back_parts, back_comm, lambda: map_channels(mixer, seed, linear)
-    ) * mode_weight()
+    mixer_t[...] = channel_map(weight[...], True)
+    map_channels(mixer_t, state, linear)
+    for i in range(C):
+        weights[0, i] = weights_t[0, i].T
+        weights[1, i] = weights_t[1, i].T
+    mixer[...] = channel_map(weight[...], False)
+
+    spectrum = reduce_scatter(comm)
+    tile = mix(weights, spectrum) * (mode_weight() * (1.0 / GRID))
+
+    def point(g):
+        expand(comm[MODES], up[...], g, rows)
+        at = slice(g * 8, g * 8 + 8)
+        linear[at] = linear[at] + dot(
+            rows[at].reshape(8 * ROWS, 256), basis_t[...]
+        ).reshape(8, ROWS, COLS)
+        for c in range(g * 8, g * 8 + 8):
+            for s in range(ROWS // SLAB):
+                x = slice(s * SLAB, s * SLAB + SLAB)
+                value = linear[c, x] + bias[c]
+                cdf = 0.5 + 0.5 * lax.erf(value * (1.0 / math.sqrt(2.0)))
+                density = jnp.exp(-0.5 * value * value) * (1.0 / math.sqrt(2.0 * math.pi))
+                slope[c, x] = (value * cdf).astype(BF16)
+                seed[c, x] = (cotangent[c, x].astype(F32) * (cdf + value * density)).astype(BF16)
+        to_columns(seed, g)
+        send_parts(back_parts, back_comm, g)
+
+    all_gather(tile, comm, lambda: reduce_scatter_sent(parts, comm), point)
+    plane_stage(back_parts, back_comm, GROUPS - 1)
+    map_channels(mixer, seed, linear)
+    cot = reduce_scatter(back_comm) * mode_weight()
 
     def meanwhile():
         weight_terms(spectrum, cot, weight_grad)
         reduce_scatter_sent(back_parts, back_comm)
-
-    all_gather(mix_back(weights, cot) * (1.0 / GRID), back_comm, meanwhile)
-    expand(back_comm[MODES], up[...], back_rows)
+        all_gather_sent(comm)
+
+    all_gather(
+        mix_back(weights, cot) * (1.0 / GRID),
+        back_comm,
+        meanwhile,
+        lambda g: expand(back_comm[MODES], up[...], g, back_rows),
+    )
+    all_gather_sent(back_comm)
 
 
 def final_kernel(
-    slope, linear, rows, basis_t_hbm, slope_out, grad_out, basis_t, grad, sems, slope_sem, load_sem
+    slope, weight_grad, linear, rows, basis_t_hbm,
+    slope_out, weight_grad_out, grad_out,
+    basis_t, grad, sems, done_sems, load_sem,
 ):
     z = lax.axis_index("narrow")
-    slope_copy = pltpu.make_async_copy(slope, slope_out, slope_sem)
-    slope_copy.start()
+    done = [
+        pltpu.make_async_copy(slope, slope_out, done_sems.at[0]),
+        pltpu.make_async_copy(weight_grad, weight_grad_out, done_sems.at[1]),
+    ]
+    for copy in done:
+        copy.start()
     load = pltpu.make_async_copy(basis_t_hbm.at[z], basis_t, load_sem)
     load.start()
     load.wait()
@@ -518,9 +553,8 @@
         copy = pltpu.make_async_copy(grad.at[:, at, :], grad_out.at[:, at, :], sems.at[s])
         copy.start()
         copies.append(copy)
-    for copy in copies:
+    for copy in copies + done:
         copy.wait()
-    slope_copy.wait()
 
 
 VMEM = pl.BlockSpec(memory_space=pltpu.VMEM)
@@ -537,18 +571,23 @@
     down_np, up_np = row_tables()
 
     def per_device(section_state, cotangent, bypass_weight, bias, spectral_weight):
-        basis_all, basis_t_all, down_all, up_all, section_state, cotangent = (
-            pltpu.with_memory_space_constraint(jnp.asarray(array), pltpu.HBM)
-            for array in (basis_np, basis_t_np, down_np, up_np, section_state, cotangent)
+        def in_hbm(array):
+            return pltpu.with_memory_space_constraint(jnp.asarray(array), pltpu.HBM)
+
+        basis_t_all = in_hbm(basis_t_np)
+        tables = (in_hbm(basis_np), basis_t_all, in_hbm(down_np), in_hbm(up_np))
+        arguments = (
+            section_state, cotangent, bypass_weight, bias, jnp.swapaxes(spectral_weight, 2, 3)
         )
         rows_shape = jax.ShapeDtypeStruct((C, ROWS, 256), BF16)
         field = jax.ShapeDtypeStruct((C, ROWS, COLS), BF16)
+        modes_shape = jax.ShapeDtypeStruct((2, C, 16, C), F32)
         wide_field = jax.ShapeDtypeStruct((C, ROWS, COLS), F32)
 
         slope, linear, rows, weight_grad = pl.pallas_call(
             main_kernel,
-            out_shape=(field, wide_field, rows_shape, jax.ShapeDtypeStruct((2, C, C, 16), F32)),
-            in_specs=[HBM, HBM, VMEM, SMEM, VMEM, HBM, HBM, HBM, HBM],
+            out_shape=(field, wide_field, rows_shape, modes_shape),
+            in_specs=[HBM] * 9,
             out_specs=(VMEM, VMEM, VMEM, VMEM),
             scratch_shapes=[
                 pltpu.VMEM((C, ROWS, COLS), BF16),
@@ -556,6 +595,10 @@
                 pltpu.VMEM((C, ROWS, COLS), BF16),
                 pltpu.VMEM((C, ROWS, 256), BF16),
                 pltpu.VMEM((C, ROWS, 256), F32),
+                pltpu.VMEM((C, C), BF16),
+                pltpu.SMEM((C,), F32),
+                pltpu.VMEM((2, C, 16, C), F32),
+                pltpu.VMEM((2, C, C, 16), F32),
                 pltpu.VMEM((COLS, 256), BF16),
                 pltpu.VMEM((256, COLS), BF16),
                 pltpu.VMEM((128, 256), BF16),
@@ -564,33 +607,30 @@
                 pltpu.VMEM((C * SLAB, C * SLAB), BF16),
                 pltpu.VMEM((GROUPS, 2, 256, 128), F32),
                 pltpu.VMEM((GROUPS, 2, 256, 128), F32),
-                pltpu.SemaphoreType.DMA((8,)),
+                pltpu.SemaphoreType.DMA((11,)),
                 *COMM_SCRATCH,
                 *COMM_SCRATCH,
             ],
             compiler_params=params(26, collective_id=0, has_side_effects=True),
             name="section",
-        )(
-            section_state, cotangent, bypass_weight, bias, spectral_weight,
-            basis_all, basis_t_all, down_all, up_all,
-        )
-
-        slope, state_grad = pl.pallas_call(
+        )(*(in_hbm(array) for array in arguments), *tables)
+
+        slope, weight_grad, state_grad = pl.pallas_call(
             final_kernel,
-            out_shape=(field, field),
-            in_specs=[VMEM, VMEM, VMEM, HBM],
-            out_specs=(HBM, HBM),
+            out_shape=(field, modes_shape, field),
+            in_specs=[VMEM, VMEM, VMEM, VMEM, HBM],
+            out_specs=(HBM, HBM, HBM),
             scratch_shapes=[
                 pltpu.VMEM((256, COLS), BF16),
                 pltpu.VMEM((C, ROWS, COLS), BF16),
                 pltpu.SemaphoreType.DMA((ROWS // SLAB,)),
-                pltpu.SemaphoreType.DMA,
+                pltpu.SemaphoreType.DMA((2,)),
                 pltpu.SemaphoreType.DMA,
             ],
             compiler_params=params(16),
             name="state_gradient",
-        )(slope, linear, rows, basis_t_all)
-        return slope, state_grad, weight_grad
+        )(slope, weight_grad, linear, rows, basis_t_all)
+        return slope, state_grad, jnp.swapaxes(weight_grad, 2, 3)
 
     split_modes = P(None, None, None, ("wide", "narrow"))
     tiles = P(None, "wide", "narrow")

time: 85.1 us -> 69.6 us (0.82)
  Pallas kernels: 80.7 us -> 68.7 us
  local copies, waits for them, and re-layouts: 3.54 us -> 0 us
    pallas_call x2, Pallas kernels: 80.7 us -> 68.7 us  [the longest x1 65.6 us: per_device(): pl.pallas_call(main_kernel, out_shape=(field, wide_field, rows_shape, mod...]
    unnamed x6 -> x0, local copies, waits for them, and re-layouts: 3.54 us -> none
where the time goes in v1:
time: 69.6 us; the launch traced here: 69.5 us
  Pallas kernels  68.7 us (99%)
  between operations  0.8 us (1%)
    pallas_call x1, Pallas kernels, per_device(): pl.pallas_call(main_kernel, out_shape=(field, wide_field, rows_shape, mod...  65.6 us
    pallas_call x1, Pallas kernels, per_device(): pl.pallas_call(final_kernel, out_shape=(field, modes_shape, field), in_sp...  3.09 us

profile of v1, /device:TPU:1, one launch (start us, length us, event | category | flops | bytes accessed | tf_op | source)
XLA Modules:
  0.0 69.5 jit_solution(7317446698774354776)
XLA Ops:
  0.6 65.6 %section.1 = (bf16[24,128,512]{2,1,0:T(8,128)(2,1)S(1)}, f32[24,128,512]{2,1,0:T(8,128)S(1)}, bf16[24,128,256]{2,1,0:T(8,128)(2,1)S(1)}, f32[2,24,16,24]{3,2,1,0:T(8,128)S(1)}) custom-call(bf16[24,128,512]{2,1,0:T(8,128)(2,1)} %state_hbm.1, bf16[24,128,512]{2,1,0:T(8,128)(2,1)} %cotangent_hbm.1, bf16[24,24]{1,0:T(8,128)(2,1)} %weight_hbm.1, f32[24]{0:T(128)} %bias_hbm.1, ...), custom_call_target="tpu_custom_call" | custom-call | tf_op jit(solution)/shard_map/section/pallas_call | solution.py:587
  66.3 3.1 %state_gradient.1 = (bf16[24,128,512]{2,1,0:T(8,128)(2,1)}, f32[2,24,16,24]{3,2,1,0:T(8,128)}, bf16[24,128,512]{2,1,0:T(8,128)(2,1)}) custom-call(bf16[24,128,512]{2,1,0:T(8,128)(2,1)S(1)} %get-tuple-element.10.slope, f32[2,24,16,24]{3,2,1,0:T(8,128)S(1)} %get-tuple-element.11.weight_grad, f32[24,128,512]{2,1,0:T(8,128)S(1)} %get-tuple-element.12.linear, ...), custom_call_target="tpu_custom_call" | custom-call | tf_op jit(solution)/shard_map/state_gradient/pallas_call | solution.py:618

commit v2 on v1

--- a/solution.py
+++ b/solution.py
@@ -140,7 +140,7 @@
     pltpu.SemaphoreType.DMA((1 + GROUPS,)),
     pltpu.SemaphoreType.DMA((2,)),
     pltpu.SemaphoreType.DMA((2,)),
-    pltpu.SemaphoreType.DMA((1 + GROUPS * PLANE,)),
+    pltpu.SemaphoreType.DMA((1 + GROUPS,)),
     pltpu.SemaphoreType.DMA((1 + GROUPS,)),
 ]
 PAIR, SLOTS, PACKED, RING, OWN, FINAL, MODES = range(7)
@@ -259,28 +259,32 @@
     ring[z] = tile
     arrived(ring.at[pl.ds(0, NARROW - 1)], ring_sems.at[1])
 
-    def chunk(g, which, j):
-        return modes.at[g, pl.ds(pl.multiple_of((which * PLANE + j) * 16, 16), 16)]
-
-    def plane_copy(g, t, j):
+    def chunk(g):
+        return modes.at[g, pl.ds(pl.multiple_of((core * PLANE + plane) * 16, 16), 16)]
+
+    def plane_copy(g, t):
         return remote(
-            chunk(g, core, j),
-            chunk(g, core, j),
+            chunk(g),
+            chunk(g),
             plane_sems.at[0],
-            plane_sems.at[1 + g * PLANE + j],
+            plane_sems.at[1 + g],
             t * 2 + core,
             z,
         )
 
-    def pair_forward(g, j):
-        return remote(
-            chunk(g, core, j),
-            chunk(g, core, j),
+    def half(g, which):
+        return modes.at[g, pl.ds(pl.multiple_of(which * 256, 256), 256)]
+
+    def forward(g):
+        arrived(modes.at[g, pl.ds(0, (PLANE - 1) * 16)], plane_sems.at[1 + g])
+        remote(
+            half(g, core),
+            half(g, core),
             pair_sems.at[0],
             pair_sems.at[1 + g],
             plane * 2 + 1 - core,
             z,
-        )
+        ).start()
 
     targets = plane_targets(plane)
     lane_group = lanes() // 32
@@ -296,23 +300,14 @@
             blocks, axis=0
         )
         for t in targets:
-            plane_copy(g, t, plane).start()
-        pair_forward(g, plane).start()
+            plane_copy(g, t).start()
     meanwhile()
-
-    def forward(g):
-        for j in reversed(targets):
-            plane_copy(g, plane, j).wait_recv()
-            pair_forward(g, j).start()
-
-    def other(g):
-        return modes.at[g, pl.ds(pl.multiple_of((1 - core) * PLANE * 16, 16), PLANE * 16)]
 
     forward(0)
     for g in range(GROUPS):
         if g + 1 < GROUPS:
             forward(g + 1)
-        arrived(other(g), pair_sems.at[1 + g])
+        arrived(half(g, 1 - core), pair_sems.at[1 + g])
         consume(g)
 
 
@@ -426,9 +421,9 @@
 def main_kernel(
     state_hbm, cotangent_hbm, weight_hbm, bias_hbm, weights_hbm,
     basis_hbm, basis_t_hbm, down_hbm, up_hbm,
-    slope, linear, back_rows, weight_grad,
+    slope, linear, back_rows, weight_grad, basis_t,
     state, cotangent, seed, rows, back, weight, bias, weights_t, weights,
-    basis, basis_t, down, up, mixer, mixer_t,
+    basis, down, up, mixer, mixer_t,
     parts, back_parts, load_sems, *comms,
 ):
     comm, back_comm = comms[: len(COMM_SCRATCH)], comms[len(COMM_SCRATCH) :]
@@ -449,7 +444,7 @@
         pltpu.make_async_copy(bias_hbm, bias, load_sems.at[9]),
         pltpu.make_async_copy(cotangent_hbm, cotangent, load_sems.at[10]),
     ]
-    for load in loads:
+    for load in loads[:5]:
         load.start()
     greet()
     for load in loads[:2]:
@@ -475,14 +470,18 @@
 
     for g in range(GROUPS):
         loads[2 + g].wait()
+        if g == GROUPS - 1:
+            for load in loads[5:]:
+                load.start()
         to_columns(state, g)
         send_parts(parts, comm, g)
     plane_stage(parts, comm, GROUPS - 1)
 
-    for load in loads[5:]:
-        load.wait()
+    loads[5].wait()
     mixer_t[...] = channel_map(weight[...], True)
     map_channels(mixer_t, state, linear)
+    for load in loads[6:]:
+        load.wait()
     for i in range(C):
         weights[0, i] = weights_t[0, i].T
         weights[1, i] = weights_t[1, i].T
@@ -528,20 +527,16 @@
 
 
 def final_kernel(
-    slope, weight_grad, linear, rows, basis_t_hbm,
+    slope, weight_grad, linear, rows, basis_t,
     slope_out, weight_grad_out, grad_out,
-    basis_t, grad, sems, done_sems, load_sem,
+    grad, sems, done_sems,
 ):
-    z = lax.axis_index("narrow")
     done = [
         pltpu.make_async_copy(slope, slope_out, done_sems.at[0]),
         pltpu.make_async_copy(weight_grad, weight_grad_out, done_sems.at[1]),
     ]
     for copy in done:
         copy.start()
-    load = pltpu.make_async_copy(basis_t_hbm.at[z], basis_t, load_sem)
-    load.start()
-    load.wait()
     size = C * SLAB
     copies = []
     for s in range(ROWS // SLAB):
@@ -574,21 +569,21 @@
         def in_hbm(array):
             return pltpu.with_memory_space_constraint(jnp.asarray(array), pltpu.HBM)
 
-        basis_t_all = in_hbm(basis_t_np)
-        tables = (in_hbm(basis_np), basis_t_all, in_hbm(down_np), in_hbm(up_np))
+        tables = [in_hbm(table) for table in (basis_np, basis_t_np, down_np, up_np)]
         arguments = (
             section_state, cotangent, bypass_weight, bias, jnp.swapaxes(spectral_weight, 2, 3)
         )
         rows_shape = jax.ShapeDtypeStruct((C, ROWS, 256), BF16)
         field = jax.ShapeDtypeStruct((C, ROWS, COLS), BF16)
         modes_shape = jax.ShapeDtypeStruct((2, C, 16, C), F32)
+        basis_shape = jax.ShapeDtypeStruct((256, COLS), BF16)
         wide_field = jax.ShapeDtypeStruct((C, ROWS, COLS), F32)
 
-        slope, linear, rows, weight_grad = pl.pallas_call(
+        slope, linear, rows, weight_grad, basis_t = pl.pallas_call(
             main_kernel,
-            out_shape=(field, wide_field, rows_shape, modes_shape),
+            out_shape=(field, wide_field, rows_shape, modes_shape, basis_shape),
             in_specs=[HBM] * 9,
-            out_specs=(VMEM, VMEM, VMEM, VMEM),
+            out_specs=(VMEM,) * 5,
             scratch_shapes=[
                 pltpu.VMEM((C, ROWS, COLS), BF16),
                 pltpu.VMEM((C, ROWS, COLS), BF16),
@@ -600,7 +595,6 @@
                 pltpu.VMEM((2, C, 16, C), F32),
                 pltpu.VMEM((2, C, C, 16), F32),
                 pltpu.VMEM((COLS, 256), BF16),
-                pltpu.VMEM((256, COLS), BF16),
                 pltpu.VMEM((128, 256), BF16),
                 pltpu.VMEM((256, 192), BF16),
                 pltpu.VMEM((C * SLAB, C * SLAB), BF16),
@@ -618,18 +612,16 @@
         slope, weight_grad, state_grad = pl.pallas_call(
             final_kernel,
             out_shape=(field, modes_shape, field),
-            in_specs=[VMEM, VMEM, VMEM, VMEM, HBM],
+            in_specs=[VMEM] * 5,
             out_specs=(HBM, HBM, HBM),
             scratch_shapes=[
-                pltpu.VMEM((256, COLS), BF16),
                 pltpu.VMEM((C, ROWS, COLS), BF16),
                 pltpu.SemaphoreType.DMA((ROWS // SLAB,)),
                 pltpu.SemaphoreType.DMA((2,)),
-                pltpu.SemaphoreType.DMA,
             ],
             compiler_params=params(16),
             name="state_gradient",
-        )(slope, weight_grad, linear, rows, basis_t_all)
+        )(slope, weight_grad, linear, rows, basis_t)
         return slope, state_grad, jnp.swapaxes(weight_grad, 2, 3)
 
     split_modes = P(None, None, None, ("wide", "narrow"))

time: 69.6 us -> 68.9 us (0.990)
  no operation moved by 1% of the time
where the time goes in v2:
time: 68.9 us
  Pallas kernels  68.2 us (99%)
    pallas_call x1, Pallas kernels, per_device(): pl.pallas_call(main_kernel, out_shape=(field, wide_field, rows_shape, mod...  65.1 us
    pallas_call x1, Pallas kernels, per_device(): pl.pallas_call(final_kernel, out_shape=(field, modes_shape, field), in_sp...  3.16 us

profile of v2, /device:TPU:1, one launch (start us, length us, event | category | flops | bytes accessed | tf_op | source)
XLA Modules:
  0.0 68.9 jit_solution(4750874654612707665)
XLA Ops:
  0.6 65.1 %section.1 = (bf16[24,128,512]{2,1,0:T(8,128)(2,1)S(1)}, f32[24,128,512]{2,1,0:T(8,128)S(1)}, bf16[24,128,256]{2,1,0:T(8,128)(2,1)S(1)}, f32[2,24,16,24]{3,2,1,0:T(8,128)S(1)}, bf16[256,512]{1,0:T(8,128)(2,1)S(1)}) custom-call(bf16[24,128,512]{2,1,0:T(8,128)(2,1)} %state_hbm.1, bf16[24,128,512]{2,1,0:T(8,128)(2,1)} %cotangent_hbm.1, ...), custom_call_target="tpu_custom_call" | custom-call | tf_op jit(solution)/shard_map/section/pallas_call | solution.py:582
  65.7 3.2 %state_gradient.1 = (bf16[24,128,512]{2,1,0:T(8,128)(2,1)}, f32[2,24,16,24]{3,2,1,0:T(8,128)}, bf16[24,128,512]{2,1,0:T(8,128)(2,1)}) custom-call(bf16[24,128,512]{2,1,0:T(8,128)(2,1)S(1)} %get-tuple-element.11.slope, f32[2,24,16,24]{3,2,1,0:T(8,128)S(1)} %get-tuple-element.12.weight_grad, f32[24,128,512]{2,1,0:T(8,128)S(1)} %get-tuple-element.13.linear, ...), custom_call_target="tpu_custom_call" | custom-call | tf_op jit(solution)/shard_map/state_gradient/pallas_call | solution.py:612

commit v3 on v2

--- a/solution.py
+++ b/solution.py
@@ -246,7 +246,7 @@
     return tile
 
 
-def all_gather(tile, comm, meanwhile, consume):
+def all_gather(tile, comm, meanwhile, consume, finish=None):
     own, ring, modes = comm[OWN], comm[FINAL], comm[MODES]
     ring_sems, plane_sems, pair_sems = comm[GATHER_RING], comm[GATHER_PLANE], comm[GATHER_PAIR]
     plane, core, z = place()
@@ -303,12 +303,15 @@
             plane_copy(g, t).start()
     meanwhile()
 
-    forward(0)
-    for g in range(GROUPS):
-        if g + 1 < GROUPS:
-            forward(g + 1)
+    for g in range(GROUPS):
+        forward(g)
+    for g in range(GROUPS):
         arrived(half(g, 1 - core), pair_sems.at[1 + g])
         consume(g)
+        if g and finish is not None:
+            finish(g - 1)
+    if finish is not None:
+        finish(GROUPS - 1)
 
 
 def all_gather_sent(comm):
@@ -496,6 +499,8 @@
         linear[at] = linear[at] + dot(
             rows[at].reshape(8 * ROWS, 256), basis_t[...]
         ).reshape(8, ROWS, COLS)
+
+    def finish(g):
         for c in range(g * 8, g * 8 + 8):
             for s in range(ROWS // SLAB):
                 x = slice(s * SLAB, s * SLAB + SLAB)
@@ -507,7 +512,7 @@
         to_columns(seed, g)
         send_parts(back_parts, back_comm, g)
 
-    all_gather(tile, comm, lambda: reduce_scatter_sent(parts, comm), point)
+    all_gather(tile, comm, lambda: reduce_scatter_sent(parts, comm), point, finish)
     plane_stage(back_parts, back_comm, GROUPS - 1)
     map_channels(mixer, seed, linear)
     cot = reduce_scatter(back_comm) * mode_weight()

time: 68.9 us -> 69.2 us (level)
  no operation moved by 1% of the time
where the time goes in v3:
time: 69.2 us; the launch traced here: 69.1 us
  Pallas kernels  68.5 us (99%)
    pallas_call x1, Pallas kernels, per_device(): pl.pallas_call(main_kernel, out_shape=(field, wide_field, rows_shape, mod...  65.3 us
    pallas_call x1, Pallas kernels, per_device(): pl.pallas_call(final_kernel, out_shape=(field, modes_shape, field), in_sp...  3.16 us

profile of v3, /device:TPU:1, one launch (start us, length us, event | category | flops | bytes accessed | tf_op | source)
XLA Modules:
  0.0 69.1 jit_solution(15203116403109034661)
XLA Ops:
  0.6 65.3 %section.1 = (bf16[24,128,512]{2,1,0:T(8,128)(2,1)S(1)}, f32[24,128,512]{2,1,0:T(8,128)S(1)}, bf16[24,128,256]{2,1,0:T(8,128)(2,1)S(1)}, f32[2,24,16,24]{3,2,1,0:T(8,128)S(1)}, bf16[256,512]{1,0:T(8,128)(2,1)S(1)}) custom-call(bf16[24,128,512]{2,1,0:T(8,128)(2,1)} %state_hbm.1, bf16[24,128,512]{2,1,0:T(8,128)(2,1)} %cotangent_hbm.1, ...), custom_call_target="tpu_custom_call" | custom-call | tf_op jit(solution)/shard_map/section/pallas_call | solution.py:587
  65.9 3.2 %state_gradient.1 = (bf16[24,128,512]{2,1,0:T(8,128)(2,1)}, f32[2,24,16,24]{3,2,1,0:T(8,128)}, bf16[24,128,512]{2,1,0:T(8,128)(2,1)}) custom-call(bf16[24,128,512]{2,1,0:T(8,128)(2,1)S(1)} %get-tuple-element.11.slope, f32[2,24,16,24]{3,2,1,0:T(8,128)S(1)} %get-tuple-element.12.weight_grad, f32[24,128,512]{2,1,0:T(8,128)S(1)} %get-tuple-element.13.linear, ...), custom_call_target="tpu_custom_call" | custom-call | tf_op jit(solution)/shard_map/state_gradient/pallas_call | solution.py:617
